TPU v7x, 512 devices: a whole 4x8x8 slice. The times are simulated.
512 devices in a mesh: group: 8 (over x, y_lo), blk: 64 (over y_hi, z, core).
Axes of the slice: x: 4, y: 8 (y_hi: 4, y_lo: 2; y = y_hi * 2 + y_lo), z: 8, core: 2. Of those that a mesh axis runs over, the one named last changes fastest.
Arguments:
- images: float32 [131072, 1152], P(('group', 'blk')), may hold values from -6 to 6
- texts: float32 [131072, 1152], P(('group', 'blk')), may hold values from -6 to 6
- image_ids: int32 [131072], P(('group', 'blk')), may hold values from 0 to 131071, as said below
- text_ids: int32 [131072], P(('group', 'blk')), may hold values from 0 to 131071, as said below
- log_scale: float32 [1], replicated, may hold values from 1.5 to 2.5
- bias: float32 [1], replicated, may hold values from -3 to -1
Outputs:
- row_loss: float32 [131072], P(('group', 'blk'))
- image_grad: float32 [131072, 1152], P(('group', 'blk'))
- text_grad: float32 [131072, 1152], P(('group', 'blk'))
Inputs may be any that keep to these rules, and one draw needn't show every extreme that they name: image_ids is a permutation of 0 to 131071. text_ids is a permutation of 0 to 131071; each text id equals the id of exactly one image, and that image's block meets the text's block in one of the 4 rounds.
All inputs are finite; a program needn't handle non-finite values.
Results may differ from a plain program's by a relative error of at most 0.005.
Values may be sent and summed in bfloat16 or wider, within the bound.
A program may use at most 64 MiB of HBM per device.

v0:
```python
import jax
import jax.numpy as jnp
from jax import lax
from jax.sharding import PartitionSpec as P


def from_behind(block, axis, distance):
    devices = range(lax.axis_size(axis))
    route = [((i - distance) % len(devices), i) for i in devices]
    return lax.ppermute(block, axis, route)


def normalize(values):
    inverse = lax.rsqrt(jnp.sum(values * values, axis=-1, keepdims=True) + 1e-06)
    return (inverse, values * inverse)


def unit_backward(inverse, unit, grad):
    return inverse * (grad - unit * jnp.sum(unit * grad, axis=-1, keepdims=True))


def pair_terms(image_half, image_keys, text_half, text_keys, scale, offset):
    dots = lax.dot_general(
        image_half, text_half, (((1,), (1,)), ((), ())), preferred_element_type=jnp.float32
    )
    logit = scale * dots + offset
    label = jnp.where(image_keys[:, None] == text_keys[None, :], 1.0, -1.0).astype(jnp.float32)
    loss = jnp.sum(jax.nn.softplus(-label * logit), axis=1)
    coeff = (-label * scale * jax.nn.sigmoid(-label * logit)).astype(jnp.bfloat16)
    return (loss, coeff)


def text_terms(coeff, image_half):
    return lax.dot_general(
        coeff, image_half, (((0,), (0,)), ((), ())), preferred_element_type=jnp.float32
    )


def back_one(values):
    return from_behind(values, "blk", -1)


def local(images, texts, image_ids, text_ids, log_scale, bias):
    scale = jnp.exp(log_scale[0])
    offset = bias[0]
    image_norm, image_unit = normalize(images)
    text_norm, text_unit = normalize(texts)
    image_half = image_unit.astype(jnp.bfloat16)
    text_half = text_unit.astype(jnp.bfloat16)
    first = from_behind((text_half, text_ids), "blk", 1)
    second = from_behind((first[0], first[1]), "blk", 1)
    third = from_behind((text_half, text_ids), "group", 1)
    met = [(text_half, text_ids), first, second, third]
    row_loss = jnp.zeros((images.shape[0],), jnp.float32)
    image_unit_grad = jnp.zeros(images.shape, jnp.float32)
    coeffs = []
    for block in met:
        loss, coeff = pair_terms(image_half, image_ids, block[0], block[1], scale, offset)
        row_loss = row_loss + loss
        image_unit_grad = image_unit_grad + jnp.dot(
            coeff, block[0], preferred_element_type=jnp.float32
        )
        coeffs.append(coeff)
    text_unit_grad = text_terms(coeffs[0], image_half)
    partial_one = text_terms(coeffs[1], image_half)
    partial_two = text_terms(coeffs[2], image_half)
    partial_hop = text_terms(coeffs[3], image_half)
    carried = from_behind(partial_two.astype(jnp.bfloat16), "blk", -1).astype(partial_two.dtype)
    text_unit_grad = text_unit_grad + back_one(carried + partial_one)
    text_unit_grad = text_unit_grad + from_behind(
        partial_hop.astype(jnp.bfloat16), "group", -1
    ).astype(partial_hop.dtype)
    image_grad = unit_backward(image_norm, image_unit, image_unit_grad)
    text_grad = unit_backward(text_norm, text_unit, text_unit_grad)
    return (row_loss, image_grad, text_grad)


def solution(mesh):
    placed = (
        P(("group", "blk"), None),
        P(("group", "blk"), None),
        P(("group", "blk")),
        P(("group", "blk")),
        P(),
        P(),
    )
    return jax.shard_map(
        local,
        mesh=mesh,
        in_specs=placed,
        out_specs=(P(("group", "blk")), P(("group", "blk"), None), P(("group", "blk"), None)),
        check_vma=False,
    )
```

profile of v0, /device:TPU:8, one launch (start us, length us, event | category | flops | bytes accessed | tf_op | source)
XLA Modules:
  0.0 120.1 jit_solution(11669812874872588175)
XLA Ops:
  0.6 3.4 %collective-permute-start.4 = (s32[256]{0:T(256)}, s32[256]{0:T(256)S(1)}, u32[]{:S(2)}, u32[]{:S(2)}) collective-permute-start(s32[256]{0:T(256)} %param.9), channel_id=1, source_target_pairs={{448,0},{0,64},{64,128},{128,192},{192,256},{256,320},{320,384},{3... | collective-permute-start | bytes 3080 | tf_op jit(solution)/shard_map/ppermute | solution.py:10
  4.1 1.9 %collective-permute-start = (s32[256]{0:T(256)}, s32[256]{0:T(256)S(1)}, u32[]{:S(2)}, u32[]{:S(2)}) collective-permute-start(s32[256]{0:T(256)} %param.9), channel_id=1, source_target_pairs={{63,0},{0,1},{1,2},{2,3},{3,4},{4,5},{5,6},{6,7},{7,8},{8,9},{9,10... | collective-permute-start | bytes 3080 | tf_op jit(solution)/shard_map/ppermute | solution.py:10
  6.0 1.4 %multiply_reduce_fusion.2 = f32[256]{0:T(256)S(1)} fusion(f32[256,1152]{1,0:T(8,128)} %param.7), kind=kLoop, calls=%fused_computation.11 | loop fusion | flops 589568 | bytes 1180672 | tf_op jit(solution)/shard_map/reduce_sum | solution.py:14
  7.5 0.1 multiply_convert_fusion
  7.6 3.6 %collective-permute-start.5 = (bf16[256,1152]{1,0:T(8,128)(2,1)S(1)}, bf16[256,1152]{1,0:T(8,128)(2,1)S(1)}, u32[]{:S(2)}, u32[]{:S(2)}) collective-permute-start(bf16[256,1152]{1,0:T(8,128)(2,1)S(1)} %multiply_convert_fusion), channel_id=1, source_target_pairs={{448,0},{0,64},{64,128},{128,192},{192,256},{256,320},{320,384},{3... | collective-permute-start | bytes 1769480 | tf_op jit(solution)/shard_map/ppermute | solution.py:10
  11.2 4.1 %collective-permute-start.1 = (bf16[256,1152]{1,0:T(8,128)(2,1)S(1)}, bf16[256,1152]{1,0:T(8,128)(2,1)S(1)}, u32[]{:S(2)}, u32[]{:S(2)}) collective-permute-start(bf16[256,1152]{1,0:T(8,128)(2,1)S(1)} %multiply_convert_fusion), channel_id=1, source_target_pairs={{63,0},{0,1},{1,2},{2,3},{3,4},{4,5},{5,6},{6,7},{7,8},{8,9},{9,10... | collective-permute-start | bytes 1769480 | tf_op jit(solution)/shard_map/ppermute | solution.py:10
  15.3 0.2 multiply_reduce_fusion.3
  17.0 0.5 fusion.9
  17.6 0.5 fusion.14
  18.0 1.3 %collective-permute-done = s32[256]{0:T(256)S(1)} collective-permute-done((s32[256]{0:T(256)}, s32[256]{0:T(256)S(1)}, u32[]{:S(2)}, u32[]{:S(2)}) %collective-permute-start) | collective-permute-done | bytes 1056 | tf_op jit(solution)/shard_map/ppermute | solution.py:10
  19.3 1.9 %collective-permute-start.2 = (s32[256]{0:T(256)S(1)}, s32[256]{0:T(256)S(1)}, u32[]{:S(2)}, u32[]{:S(2)}) collective-permute-start(s32[256]{0:T(256)S(1)} %collective-permute-done), channel_id=1, source_target_pairs={{63,0},{0,1},{1,2},{2,3},{3,4},{4,5},{5,6},{6,7},{7,8},{8,9},{9,10... | collective-permute-start | bytes 3080 | tf_op jit(solution)/shard_map/ppermute | solution.py:10
  21.2 10.3 %collective-permute-done.1 = bf16[256,1152]{1,0:T(8,128)(2,1)S(1)} collective-permute-done((bf16[256,1152]{1,0:T(8,128)(2,1)S(1)}, bf16[256,1152]{1,0:T(8,128)(2,1)S(1)}, u32[]{:S(2)}, u32[]{:S(2)}) %collective-permute-start.1) | collective-permute-done | bytes 589856 | tf_op jit(solution)/shard_map/ppermute | solution.py:10
  31.5 1.9 %collective-permute-start.3 = (bf16[256,1152]{1,0:T(8,128)(2,1)S(1)}, bf16[256,1152]{1,0:T(8,128)(2,1)S(1)}, u32[]{:S(2)}, u32[]{:S(2)}) collective-permute-start(bf16[256,1152]{1,0:T(8,128)(2,1)S(1)} %collective-permute-done.1), channel_id=1, source_target_pairs={{63,0},{0,1},{1,2},{2,3},{3,4},{4,5},{5,6},{6,7},{7,8},{8,9},{9,10... | collective-permute-start | bytes 1769480 | tf_op jit(solution)/shard_map/ppermute | solution.py:10
  33.4 0.5 fusion.12
  34.0 0.4 convolution_convert_fusion
  34.4 26.5 %collective-permute-start.8 = (bf16[256,1152]{1,0:T(8,128)(2,1)S(1)}, bf16[256,1152]{1,0:T(8,128)(2,1)S(1)}, u32[]{:S(2)}, u32[]{:S(2)}) collective-permute-start(bf16[256,1152]{1,0:T(8,128)(2,1)S(1)} %convolution_convert_fusion), channel_id=1, source_target_pairs={{64,0},{128,64},{192,128},{256,192},{320,256},{384,320},{448,384},... | collective-permute-start | bytes 1769480 | tf_op jit(solution)/shard_map/ppermute | solution.py:10
  60.9 0.5 fusion.16
  61.4 0.5 fusion.11
  61.9 0.4 convolution_convert_fusion.1
  62.3 7.6 %collective-permute-start.6 = (bf16[256,1152]{1,0:T(8,128)(2,1)S(1)}, bf16[256,1152]{1,0:T(8,128)(2,1)S(1)}, u32[]{:S(2)}, u32[]{:S(2)}) collective-permute-start(bf16[256,1152]{1,0:T(8,128)(2,1)S(1)} %convolution_convert_fusion.1), channel_id=1, source_target_pairs={{1,0},{2,1},{3,2},{4,3},{5,4},{6,5},{7,6},{8,7},{9,8},{10,9},{11,1... | collective-permute-start | bytes 1769480 | tf_op jit(solution)/shard_map/ppermute | solution.py:10
  69.9 0.5 fusion.10
  70.5 0.4 fusion.15
  70.9 0.5 convolution_add_fusion.1
  71.3 12.3 %collective-permute-done.6 = bf16[256,1152]{1,0:T(8,128)(2,1)S(1)} collective-permute-done((bf16[256,1152]{1,0:T(8,128)(2,1)S(1)}, bf16[256,1152]{1,0:T(8,128)(2,1)S(1)}, u32[]{:S(2)}, u32[]{:S(2)}) %collective-permute-start.6) | collective-permute-done | bytes 589856 | tf_op jit(solution)/shard_map/ppermute | solution.py:10
  83.7 0.1 convert_add_fusion.1
  83.8 8.1 %collective-permute-start.7 = (f32[256,1152]{1,0:T(8,128)S(1)}, f32[256,1152]{1,0:T(8,128)S(1)}, u32[]{:S(2)}, u32[]{:S(2)}) collective-permute-start(f32[256,1152]{1,0:T(8,128)S(1)} %convert_add_fusion.1), channel_id=1, source_target_pairs={{1,0},{2,1},{3,2},{4,3},{5,4},{6,5},{7,6},{8,7},{9,8},{10,9},{11,1... | collective-permute-start | bytes 3538952 | tf_op jit(solution)/shard_map/ppermute | solution.py:10
  91.9 0.6 add_add_fusion
  92.5 0.7 multiply_reduce_fusion.1
  93.1 1.3 %subtract_multiply_fusion.1 = f32[256,1152]{1,0:T(8,128)} fusion(f32[256,1152]{1,0:T(8,128)S(1)} %get-tuple-element.12, f32[256,1152]{1,0:T(8,128)S(1)} %copy-done, f32[256]{0:T(256)S(1)} %get-tuple-element.11, f32[256]{0:T(256)S(1)} %add_rsqrt_fusion.1), kind=kLoop, calls=%fused_computation.9 | loop fusion | flops 1179648 | bytes 3540992 | tf_op jit(solution)/shard_map/mul | solution.py:19
  94.4 23.8 %collective-permute-done.7 = f32[256,1152]{1,0:T(8,128)S(1)} collective-permute-done((f32[256,1152]{1,0:T(8,128)S(1)}, f32[256,1152]{1,0:T(8,128)S(1)}, u32[]{:S(2)}, u32[]{:S(2)}) %collective-permute-start.7) | collective-permute-done | bytes 1179680 | tf_op jit(solution)/shard_map/ppermute | solution.py:10
  118.2 0.6 multiply_reduce_fusion
  118.8 1.3 %subtract_multiply_fusion = f32[256,1152]{1,0:T(8,128)} fusion(f32[256,1152]{1,0:T(8,128)S(1)} %copy-done.1, f32[256]{0:T(256)S(1)} %get-tuple-element.13, f32[256]{0:T(256)S(1)} %add_rsqrt_fusion, bf16[256,1152]{1,0:T(8,128)(2,1)S(1)} %collective-permute-done.8, f32[256,1152]{1,0:T(8,128)S(1)} %get-tuple-element.14, f32[256,1152]{1,0:T(8,128)S(1)} %collective-permute-done.7), kind=kLoop, calls=%fused_computation.5 | loop fusion | flops 2064384 | bytes 5310464 | tf_op jit(solution)/shard_map/mul | solution.py:19
  (16 shorter events, 0.2 us)
Async XLA Ops:
  0.6 6.8 %copy-start.1 = (f32[256,1152]{1,0:T(8,128)S(1)}, f32[256,1152]{1,0:T(8,128)}, u32[]{:S(2)}) copy-start(f32[256,1152]{1,0:T(8,128)} %param.7) | copy-start | bytes 3538948
  0.6 32.8 %collective-permute-start.4 = (s32[256]{0:T(256)}, s32[256]{0:T(256)S(1)}, u32[]{:S(2)}, u32[]{:S(2)}) collective-permute-start(s32[256]{0:T(256)} %param.9), channel_id=1, source_target_pairs={{448,0},{0,64},{64,128},{128,192},{192,256},{256,320},{320,384},{3... | collective-permute-start | bytes 3080 | tf_op jit(solution)/shard_map/ppermute | solution.py:10
  4.1 15.3 %collective-permute-start = (s32[256]{0:T(256)}, s32[256]{0:T(256)S(1)}, u32[]{:S(2)}, u32[]{:S(2)}) collective-permute-start(s32[256]{0:T(256)} %param.9), channel_id=1, source_target_pairs={{63,0},{0,1},{1,2},{2,3},{3,4},{4,5},{5,6},{6,7},{7,8},{8,9},{9,10... | collective-permute-start | bytes 3080 | tf_op jit(solution)/shard_map/ppermute | solution.py:10
  7.4 7.9 %copy-start = (f32[256,1152]{1,0:T(8,128)S(1)}, f32[256,1152]{1,0:T(8,128)}, u32[]{:S(2)}) copy-start(f32[256,1152]{1,0:T(8,128)} %param.6) | copy-start | bytes 3538948
  7.6 25.8 %collective-permute-start.5 = (bf16[256,1152]{1,0:T(8,128)(2,1)S(1)}, bf16[256,1152]{1,0:T(8,128)(2,1)S(1)}, u32[]{:S(2)}, u32[]{:S(2)}) collective-permute-start(bf16[256,1152]{1,0:T(8,128)(2,1)S(1)} %multiply_convert_fusion), channel_id=1, source_target_pairs={{448,0},{0,64},{64,128},{128,192},{192,256},{256,320},{320,384},{3... | collective-permute-start | bytes 1769480 | tf_op jit(solution)/shard_map/ppermute | solution.py:10
  11.2 20.3 %collective-permute-start.1 = (bf16[256,1152]{1,0:T(8,128)(2,1)S(1)}, bf16[256,1152]{1,0:T(8,128)(2,1)S(1)}, u32[]{:S(2)}, u32[]{:S(2)}) collective-permute-start(bf16[256,1152]{1,0:T(8,128)(2,1)S(1)} %multiply_convert_fusion), channel_id=1, source_target_pairs={{63,0},{0,1},{1,2},{2,3},{3,4},{4,5},{5,6},{6,7},{7,8},{8,9},{9,10... | collective-permute-start | bytes 1769480 | tf_op jit(solution)/shard_map/ppermute | solution.py:10
  15.5 1.5 %copy-start.2 = (s32[256]{0:T(256)S(1)}, s32[256]{0:T(256)}, u32[]{:S(2)}) copy-start(s32[256]{0:T(256)} %param.8) | copy-start | bytes 3076
  15.5 1.5 %copy-start.3 = (s32[256]{0:T(256)S(1)}, s32[256]{0:T(256)}, u32[]{:S(2)}) copy-start(s32[256]{0:T(256)} %param.9) | copy-start | bytes 3076
  19.3 42.1 %collective-permute-start.2 = (s32[256]{0:T(256)S(1)}, s32[256]{0:T(256)S(1)}, u32[]{:S(2)}, u32[]{:S(2)}) collective-permute-start(s32[256]{0:T(256)S(1)} %collective-permute-done), channel_id=1, source_target_pairs={{63,0},{0,1},{1,2},{2,3},{3,4},{4,5},{5,6},{6,7},{7,8},{8,9},{9,10... | collective-permute-start | bytes 3080 | tf_op jit(solution)/shard_map/ppermute | solution.py:10
  31.5 29.9 %collective-permute-start.3 = (bf16[256,1152]{1,0:T(8,128)(2,1)S(1)}, bf16[256,1152]{1,0:T(8,128)(2,1)S(1)}, u32[]{:S(2)}, u32[]{:S(2)}) collective-permute-start(bf16[256,1152]{1,0:T(8,128)(2,1)S(1)} %collective-permute-done.1), channel_id=1, source_target_pairs={{63,0},{0,1},{1,2},{2,3},{3,4},{4,5},{5,6},{6,7},{7,8},{8,9},{9,10... | collective-permute-start | bytes 1769480 | tf_op jit(solution)/shard_map/ppermute | solution.py:10
  34.4 60.0 %collective-permute-start.8 = (bf16[256,1152]{1,0:T(8,128)(2,1)S(1)}, bf16[256,1152]{1,0:T(8,128)(2,1)S(1)}, u32[]{:S(2)}, u32[]{:S(2)}) collective-permute-start(bf16[256,1152]{1,0:T(8,128)(2,1)S(1)} %convolution_convert_fusion), channel_id=1, source_target_pairs={{64,0},{128,64},{192,128},{256,192},{320,256},{384,320},{448,384},... | collective-permute-start | bytes 1769480 | tf_op jit(solution)/shard_map/ppermute | solution.py:10
  62.3 21.3 %collective-permute-start.6 = (bf16[256,1152]{1,0:T(8,128)(2,1)S(1)}, bf16[256,1152]{1,0:T(8,128)(2,1)S(1)}, u32[]{:S(2)}, u32[]{:S(2)}) collective-permute-start(bf16[256,1152]{1,0:T(8,128)(2,1)S(1)} %convolution_convert_fusion.1), channel_id=1, source_target_pairs={{1,0},{2,1},{3,2},{4,3},{5,4},{6,5},{7,6},{8,7},{9,8},{10,9},{11,1... | collective-permute-start | bytes 1769480 | tf_op jit(solution)/shard_map/ppermute | solution.py:10
  83.8 34.4 %collective-permute-start.7 = (f32[256,1152]{1,0:T(8,128)S(1)}, f32[256,1152]{1,0:T(8,128)S(1)}, u32[]{:S(2)}, u32[]{:S(2)}) collective-permute-start(f32[256,1152]{1,0:T(8,128)S(1)} %convert_add_fusion.1), channel_id=1, source_target_pairs={{1,0},{2,1},{3,2},{4,3},{5,4},{6,5},{7,6},{8,7},{9,8},{10,9},{11,1... | collective-permute-start | bytes 3538952 | tf_op jit(solution)/shard_map/ppermute | solution.py:10
where the time goes:
time: 121 us; the launch traced here: 120 us
  starting transfers between devices  59.1 us (49%)
  waiting for transfers between devices  47.7 us (39%)
  matrix products  5.98 us (5%)
  other arithmetic  5.17 us (4%)
  between operations  2.2 us (2%)
    ppermute x9, starting transfers between devices, from_behind(): return lax.ppermute(block, axis, route)  59.1 us
    ppermute x9, waiting for transfers between devices, from_behind(): return lax.ppermute(block, axis, route)  47.7 us
    mul x2, other arithmetic, unit_backward(): inverse * (grad - unit * jnp.sum(unit * grad, axis=-1, keepdims=True))  2.61 us
  transfers between devices with their start and end apart: 9, of which 4 were waited for; matrix products, arithmetic and copies ran while one was open for 8% of the time, Pallas kernels for 0%

commit v1 on v0

v1 whole, which is shorter than its diff:
```python
import functools

import jax
import jax.numpy as jnp
from jax import lax
from jax.experimental import pallas as pl
from jax.experimental.pallas import tpu as pltpu
from jax.sharding import PartitionSpec as P

MESH = pl.DeviceIdType.MESH
ROWS = 256
D = 1152
N_Z = 8
N_YHI = 4
N_GROUP = 8
STRIP = ROWS // N_Z
CHUNK = 64
N_CHUNK = ROWS // CHUNK
TILE = 384
F32 = jnp.float32
BF16 = jnp.bfloat16


def rows_of(ref, start, count):
    return ref.at[pl.ds(start, count)]


def kernel(
    images, texts, image_ids, text_ids, log_scale, bias,
    loss_out, image_out, text_out,
    im, tx, ih, th, inv_i, inv_t, acc_i, acc_t, loss_acc, col_i, col_t, ids,
    t1, t2, tg, i1, i2, ig, relay_t, relay_i, ids_in,
    load_sem, send_sem, chunk_send, chunk_recv, block_recv, ids_send, ids_recv, strip_send, ready_next, ready_strip, ready_wrap,
):
    g = lax.axis_index("group")
    k = lax.axis_index("blk")
    core = lax.rem(k, 2)
    z = lax.rem(k // 2, N_Z)
    yhi = k // (2 * N_Z)
    first, last = z == 0, z == N_Z - 1

    def at(yh, zz, cc):
        return (g, (lax.rem(yh + N_YHI, N_YHI) * N_Z + zz) * 2 + cc)

    g_next = (lax.rem(g + 1, N_GROUP), k)
    g_prev = (lax.rem(g + N_GROUP - 1, N_GROUP), k)
    partner = (g, k + 1 - 2 * core)
    wrap_next = at(yhi + 1, 0, core)
    wrap_prev = at(yhi - 1, N_Z - 1, core)
    k_next = (g, lax.rem(k + 2, 2 * N_Z * N_YHI))
    k_prev = (g, lax.rem(k + 2 * N_Z * N_YHI - 2, 2 * N_Z * N_YHI))

    barrier = pltpu.get_barrier_semaphore()

    def tell(device):
        pl.semaphore_signal(barrier, inc=1, device_id=device, device_id_type=MESH)

    tell(g_next)
    tell(g_prev)
    tell(partner)

    loads = []
    for c in range(N_CHUNK):
        for a, (src, dst) in enumerate(((texts, tx), (images, im))):
            rows = pl.ds(c * CHUNK, CHUNK)
            copy = pltpu.make_async_copy(src.at[rows], dst.at[rows], load_sem.at[a, c])
            copy.start()
            loads.append(copy)

    @pl.when(jnp.logical_not(last))
    def _():
        tell(k_next)
        tell(at(yhi, N_Z - 1, core))
        tell(wrap_prev)

    @pl.when(last)
    def _():
        tell(at(yhi + 1, N_Z - 1, core))

    @pl.when(first)
    def _():
        for s in range(N_Z):
            tell(at(yhi - 1, s, core))
        for s in range(1, N_Z):
            tell(at(yhi, s, core))

    ids[...] = jnp.concatenate(
        [text_ids[...], image_ids[...], jnp.zeros((6, ROWS), jnp.int32)], axis=0
    )
    col_t[...] = jnp.broadcast_to(text_ids[...].astype(F32), (128, ROWS)).T
    col_i[...] = jnp.broadcast_to(image_ids[...].astype(F32), (128, ROWS)).T
    scale = jnp.exp(jnp.full((1, 1), log_scale[0], F32))
    offset = bias[0]

    def remote(src, dst, send, recv, device):
        return pltpu.make_async_remote_copy(
            src_ref=src, dst_ref=dst, send_sem=send, recv_sem=recv,
            device_id=device, device_id_type=MESH,
        )

    def group_text(c):
        return remote(rows_of(th, c * CHUNK, CHUNK), rows_of(tg, c * CHUNK, CHUNK),
                      chunk_send.at[0, c], chunk_recv.at[0, c], g_next)

    def group_image(c):
        return remote(rows_of(ih, c * CHUNK, CHUNK), rows_of(ig, c * CHUNK, CHUNK),
                      chunk_send.at[1, c], chunk_recv.at[1, c], g_prev)

    half = ROWS // 2

    def next_text(part):
        return remote(rows_of(th, part * half, half), rows_of(t2, part * half, half),
                      send_sem.at[part], block_recv.at[0], k_next)

    def prev_image(part):
        return remote(rows_of(ih, part * half, half), rows_of(i2, part * half, half),
                      send_sem.at[2 + part], block_recv.at[1], k_prev)

    def strip_text(s):
        return remote(rows_of(th, s * STRIP, STRIP), relay_t, strip_send.at[s], block_recv.at[2], at(yhi, s, core))

    def strip_image(s):
        return remote(rows_of(ih, s * STRIP, STRIP), relay_i, strip_send.at[s], block_recv.at[3], at(yhi, s, core))

    mine = pl.multiple_of(z * STRIP, STRIP)
    pass_text = remote(relay_t, rows_of(t2, mine, STRIP), send_sem.at[4], block_recv.at[0], wrap_next)
    pass_image = remote(relay_i, rows_of(i2, mine, STRIP), send_sem.at[5], block_recv.at[1], wrap_prev)
    end = (N_Z - 1) * STRIP
    own_text = remote(rows_of(th, end, STRIP), rows_of(t2, end, STRIP), send_sem.at[4], block_recv.at[0], wrap_next)
    own_image = remote(rows_of(ih, 0, STRIP), rows_of(i2, 0, STRIP), send_sem.at[5], block_recv.at[1], wrap_prev)

    core_text = remote(th, t1, send_sem.at[6], block_recv.at[4], partner)
    core_image = remote(ih, i1, send_sem.at[6], block_recv.at[5], partner)
    on_text = remote(t2, t1, send_sem.at[7], block_recv.at[4], partner)
    on_image = remote(i2, i1, send_sem.at[7], block_recv.at[5], partner)

    def send_ids(slot, device, src=ids):
        return remote(src, ids_in.at[slot], ids_send.at[slot], ids_recv.at[slot], device)

    ids_next, ids_prev = send_ids(2, k_next), send_ids(3, k_prev)
    ids_copies = [send_ids(0, g_next), send_ids(1, g_prev), send_ids(4, partner)]
    ids_on_text = send_ids(5, partner, ids_in.at[2])
    ids_on_image = send_ids(5, partner, ids_in.at[3])

    def normalize(c, raw, half_ref, inv_ref):
        rows = pl.ds(c * CHUNK, CHUNK)
        values = raw[rows, :]
        inv = lax.rsqrt(jnp.sum(values * values, axis=-1, keepdims=True) + 1e-06)
        half_ref[rows, :] = (values * inv).astype(BF16)
        inv_ref[rows, :] = jnp.broadcast_to(inv, (CHUNK, 128))

    for c in range(N_CHUNK):
        loads[2 * c].wait()
        normalize(c, tx, th, inv_t)
        if c == 0:
            pl.semaphore_wait(
                barrier, 4 + 2 * (z > 0).astype(jnp.int32) + 15 * last.astype(jnp.int32)
            )
        if c < 2:
            group_text(c).start()

        @pl.when(last)
        def _():
            for s in range(c * CHUNK // STRIP, (c + 1) * CHUNK // STRIP):
                if s < N_Z - 1:
                    strip_text(s).start()
                else:
                    own_text.start()

        if c == 0:
            @pl.when(z > 0)
            def _():
                pl.semaphore_signal(ready_next, inc=1, device_id=k_prev, device_id_type=MESH)
                pl.semaphore_signal(ready_strip.at[z], inc=1, device_id=at(yhi, 0, core), device_id_type=MESH)

            @pl.when(last)
            def _():
                for s in range(N_Z - 1):
                    pl.semaphore_signal(ready_wrap, inc=1, device_id=at(yhi + 1, s, core), device_id_type=MESH)

        loads[2 * c + 1].wait()
        normalize(c, im, ih, inv_i)
        if c < 2:
            group_image(c).start()

    for copy in ids_copies:
        copy.start()

    @pl.when(core == 0)
    def _():
        core_text.start()

    @pl.when(core == 1)
    def _():
        core_image.start()

    @pl.when(z > 0)
    def _():
        ids_prev.start()
        prev_image(0).start()
        prev_image(1).start()

    @pl.when(jnp.logical_not(last))
    def _():
        pl.semaphore_wait(ready_next, 1)
        ids_next.start()
        next_text(0).start()

    @pl.when(last)
    def _():
        ids_next.start()

    @pl.when(jnp.logical_not(last) & (z > 0))
    def _():
        next_text(1).start()

    def side(own_half, own_col, other, start, count, other_ids, acc, loss, fresh=False):
        block = other[pl.ds(start, count), :]
        dots = lax.dot_general(
            own_half[...], block, (((1,), (1,)), ((), ())), preferred_element_type=F32
        )
        logit = scale * dots + offset
        same = own_col[:, 0:1] == other_ids.astype(F32)
        u = jnp.where(same, -logit, logit)
        e = jnp.exp(-jnp.abs(u))
        coeff = jnp.where(same, -scale, scale) * (jnp.where(u >= 0, 1.0, e) / (1.0 + e))
        coeff = coeff.astype(BF16)
        if loss is not None:
            terms = jnp.maximum(u, 0.0) + jnp.log1p(e)
            terms = jnp.sum(terms, axis=1, keepdims=True)
            terms = jnp.broadcast_to(terms, (ROWS, 128))
            loss[...] = terms if fresh else loss[...] + terms

        def add(t, carry):
            cols = pl.ds(pl.multiple_of(t * TILE, 128), TILE)
            term = jnp.dot(coeff, other[pl.ds(start, count), cols], preferred_element_type=F32)
            acc[:, cols] = term if fresh else acc[:, cols] + term
            return carry

        lax.fori_loop(0, D // TILE, add, 0)

    def image_side(block, text_row, start=0, count=ROWS, fresh=False):
        side(ih, col_i, block, start, count, text_row, acc_i, loss_acc, fresh)

    def text_side(block, image_row, start=0, count=ROWS, fresh=False):
        side(th, col_t, block, start, count, image_row, acc_t, None, fresh)

    image_side(th, ids[0:1, :], fresh=True)

    @pl.when(first)
    def _():
        for s in range(1, 5):
            pl.semaphore_wait(ready_strip.at[s], 1)
            strip_image(s).start()
        next_text(1).start()

    text_side(ih, ids[1:2, :], fresh=True)

    send_ids(4, partner).wait_recv()

    @pl.when(core == 0)
    def _():
        core_image.wait_recv()
        text_side(i1, ids_in[4, 1:2, :])

    @pl.when(core == 1)
    def _():
        core_text.wait_recv()
        image_side(t1, ids_in[4, 0:1, :])

    @pl.when(first)
    def _():
        for s in range(5, N_Z):
            pl.semaphore_wait(ready_strip.at[s], 1)
            strip_image(s).start()

    @pl.when(z > 0)
    def _():
        strip_image(0).wait_recv()

    @pl.when(jnp.logical_not(last))
    def _():
        pl.semaphore_wait(ready_wrap, 1)

    @pl.when(z > 0)
    def _():
        pass_image.start()

    @pl.when(first)
    def _():
        own_image.start()
        ids_prev.start()

    for c in range(2, N_CHUNK):
        group_image(c).start()

    @pl.when(jnp.logical_not(last))
    def _():
        strip_text(0).wait_recv()
        pass_text.start()

    for c in range(2, N_CHUNK):
        group_text(c).start()

    whole_text = remote(th, t2, send_sem.at[0], block_recv.at[0], k_next)
    whole_image = remote(ih, i2, send_sem.at[2], block_recv.at[1], k_prev)
    ids_prev.wait_recv()
    whole_image.wait_recv()

    @pl.when(core == 0)
    def _():
        ids_on_image.start()
        on_image.start()

    text_side(i2, ids_in[3, 1:2, :])
    ids_next.wait_recv()
    whole_text.wait_recv()

    @pl.when(core == 1)
    def _():
        ids_on_text.start()
        on_text.start()

    image_side(t2, ids_in[2, 0:1, :])
    ids_on_text.wait_recv()

    @pl.when(core == 0)
    def _():
        on_text.wait_recv()
        image_side(t1, ids_in[5, 0:1, :])

    @pl.when(core == 1)
    def _():
        on_image.wait_recv()
        text_side(i1, ids_in[5, 1:2, :])

    ids_copies[0].wait_recv()
    ids_copies[1].wait_recv()
    for c in range(N_CHUNK):
        here = c * CHUNK
        group_text(c).wait_recv()
        image_side(tg, ids_in[0, 0:1, here:here + CHUNK], here, CHUNK)
        group_image(c).wait_recv()
        text_side(ig, ids_in[1, 1:2, here:here + CHUNK], here, CHUNK)

    def backward(raw, inv_ref, acc, out):
        def step(r, carry):
            rows = pl.ds(pl.multiple_of(r * 32, 32), 32)
            inv = inv_ref[rows, 0:1]
            unit = raw[rows, :] * inv
            grad = acc[rows, :]
            out[rows, :] = inv * (grad - unit * jnp.sum(unit * grad, axis=-1, keepdims=True))
            return carry

        lax.fori_loop(0, ROWS // 32, step, 0)

    backward(im, inv_i, acc_i, image_out)
    backward(tx, inv_t, acc_t, text_out)
    loss_out[...] = loss_acc[...].T[0:1, :]

    for c in range(N_CHUNK):
        group_text(c).wait_send()
        group_image(c).wait_send()
    for copy in ids_copies:
        copy.wait_send()
    ids_next.wait_send()
    ids_prev.wait_send()
    ids_on_text.wait_send()
    core_text.wait_send()
    on_text.wait_send()

    @pl.when(z > 0)
    def _():
        prev_image(0).wait_send()
        prev_image(1).wait_send()

    @pl.when(jnp.logical_not(last))
    def _():
        next_text(0).wait_send()
        next_text(1).wait_send()

    pass_text.wait_send()
    pass_image.wait_send()

    @pl.when(last)
    def _():
        for s in range(N_Z - 1):
            strip_text(s).wait_send()

    @pl.when(first)
    def _():
        for s in range(1, N_Z):
            strip_image(s).wait_send()


def local(images, texts, image_ids, text_ids, log_scale, bias):
    block = pltpu.VMEM((ROWS, D), BF16)
    wide = pltpu.VMEM((ROWS, D), F32)
    lanes = pltpu.VMEM((ROWS, 128), F32)
    dma, plain = pltpu.SemaphoreType.DMA, pltpu.SemaphoreType.REGULAR
    vmem = pl.BlockSpec(memory_space=pltpu.VMEM)
    smem = pl.BlockSpec(memory_space=pltpu.SMEM)
    hbm = pl.BlockSpec(memory_space=pl.ANY)
    row_loss, image_grad, text_grad = pl.pallas_call(
        kernel,
        out_shape=(
            jax.ShapeDtypeStruct((1, ROWS), F32),
            jax.ShapeDtypeStruct((ROWS, D), F32),
            jax.ShapeDtypeStruct((ROWS, D), F32),
        ),
        in_specs=[hbm, hbm, vmem, vmem, smem, smem],
        out_specs=(vmem, vmem, vmem),
        scratch_shapes=[
            wide, wide, block, block, lanes, lanes, wide, wide, lanes, lanes, lanes,
            pltpu.VMEM((8, ROWS), jnp.int32),
            block, block, block, block, block, block,
            pltpu.VMEM((STRIP, D), BF16), pltpu.VMEM((STRIP, D), BF16),
            pltpu.VMEM((6, 8, ROWS), jnp.int32),
            dma((2, N_CHUNK)), dma((8,)), dma((2, N_CHUNK)), dma((2, N_CHUNK)), dma((6,)),
            dma((6,)), dma((6,)), dma((N_Z,)), plain, plain((N_Z,)), plain,
        ],
        compiler_params=pltpu.CompilerParams(
            collective_id=0, has_side_effects=True, vmem_limit_bytes=48 * 1024 * 1024
        ),
    )(images, texts, image_ids.reshape(1, ROWS), text_ids.reshape(1, ROWS), log_scale, bias)
    return row_loss.reshape(ROWS), image_grad, text_grad


def solution(mesh):
    rows, wide = P(("group", "blk")), P(("group", "blk"), None)
    return jax.shard_map(
        local,
        mesh=mesh,
        in_specs=(wide, wide, rows, rows, P(), P()),
        out_specs=(rows, wide, wide),
        check_vma=False,
    )
```

time: 121 us -> 65.3 us (0.54)
  the two profiles are of different devices: /device:TPU:8 before, /device:TPU:6 now
where the time goes in v1:
time: 65.3 us; the launch traced here: 65 us
  Pallas kernels  56.6 us (87%)
  local copies, waits for them, and re-layouts  6.48 us (10%)
  between operations  1.94 us (3%)
    pallas_call x1, Pallas kernels, local(): pl.pallas_call(kernel, out_shape=(jax.ShapeDtypeStruct((1, ROWS), F32), j...  56.6 us
    unnamed x11, local copies, waits for them, and re-layouts  6.48 us

profile of v1, /device:TPU:6, one launch (start us, length us, event | category | flops | bytes accessed | tf_op | source)
XLA Modules:
  0.0 65.0 jit_solution(15213326910803446312)
XLA Ops:
  1.9 0.0 copy-start
  1.9 1.3 %copy-done = f32[256,1152]{1,0:T(8,128)S(1)} copy-done((f32[256,1152]{1,0:T(8,128)S(1)}, f32[256,1152]{1,0:T(8,128)}, u32[]{:S(2)}) %copy-start) | copy-done | bytes 1179672
  3.2 0.0 copy-start.1
  3.2 1.3 %copy-done.1 = f32[256,1152]{1,0:T(8,128)S(1)} copy-done((f32[256,1152]{1,0:T(8,128)S(1)}, f32[256,1152]{1,0:T(8,128)}, u32[]{:S(2)}) %copy-start.1) | copy-done | bytes 1179672
  4.5 0.0 copy-start.2
  4.5 0.7 %copy-done.2 = s32[256]{0:T(256)S(1)} copy-done((s32[256]{0:T(256)S(1)}, s32[256]{0:T(256)}, u32[]{:S(2)}) %copy-start.2) | copy-done | bytes 1048
  5.1 0.0 copy-start.3
  5.1 0.7 %copy-done.3 = s32[256]{0:T(256)S(1)} copy-done((s32[256]{0:T(256)S(1)}, s32[256]{0:T(256)}, u32[]{:S(2)}) %copy-start.3) | copy-done | bytes 1048
  5.8 56.6 %shard_map.85 = (f32[1,256]{1,0:T(1,128)S(1)}, f32[256,1152]{1,0:T(8,128)S(1)}, f32[256,1152]{1,0:T(8,128)S(1)}) custom-call(f32[256,1152]{1,0:T(8,128)S(1)} %copy-done, f32[256,1152]{1,0:T(8,128)S(1)} %copy-done.1, s32[1,256]{1,0:T(1,128)S(1)} %bitcast.3, s32[1,256]{1,0:T(1,128)S(1)} %bitcast.4, f32[1]{0:T(128)S(6)} %copy.12.log_scale, f32[1]{0:T(128)S(6)} %copy.13.bias), custom_call_target="tpu_custom_call" | custom-call | tf_op jit(solution)/shard_map/pallas_call | solution.py:404
  62.4 0.6 copy.14
  63.0 1.0 %copy.15 = f32[256,1152]{1,0:T(8,128)} copy(f32[256,1152]{1,0:T(8,128)S(1)} %get-tuple-element.13) | data formatting | bytes 2359296
  64.0 1.0 %copy.16 = f32[256,1152]{1,0:T(8,128)} copy(f32[256,1152]{1,0:T(8,128)S(1)} %get-tuple-element.14) | data formatting | bytes 2359296
Async XLA Ops:
  1.9 1.3 %copy-start = (f32[256,1152]{1,0:T(8,128)S(1)}, f32[256,1152]{1,0:T(8,128)}, u32[]{:S(2)}) copy-start(f32[256,1152]{1,0:T(8,128)} %images.1) | copy-start | bytes 3538948
  3.2 1.3 %copy-start.1 = (f32[256,1152]{1,0:T(8,128)S(1)}, f32[256,1152]{1,0:T(8,128)}, u32[]{:S(2)}) copy-start(f32[256,1152]{1,0:T(8,128)} %texts.1) | copy-start | bytes 3538948
  4.5 0.7 %copy-start.2 = (s32[256]{0:T(256)S(1)}, s32[256]{0:T(256)}, u32[]{:S(2)}) copy-start(s32[256]{0:T(256)} %param.8) | copy-start | bytes 3076
  5.1 0.7 %copy-start.3 = (s32[256]{0:T(256)S(1)}, s32[256]{0:T(256)}, u32[]{:S(2)}) copy-start(s32[256]{0:T(256)} %param.9) | copy-start | bytes 3076

commit v2 on v1

--- a/solution.py
+++ b/solution.py
@@ -16,6 +16,8 @@
 STRIP = ROWS // N_Z
 CHUNK = 64
 N_CHUNK = ROWS // CHUNK
+N_FIRST_TEXT = 1
+N_FIRST_IMAGE = 3
 TILE = 384
 F32 = jnp.float32
 BF16 = jnp.bfloat16
@@ -27,10 +29,10 @@
 
 def kernel(
     images, texts, image_ids, text_ids, log_scale, bias,
-    loss_out, image_out, text_out,
-    im, tx, ih, th, inv_i, inv_t, acc_i, acc_t, loss_acc, col_i, col_t, ids,
+    im, tx, inv_i, inv_t, acc_i, acc_t, loss_acc,
+    ih, th, col_i, col_t, id_rows, ids,
     t1, t2, tg, i1, i2, ig, relay_t, relay_i, ids_in,
-    load_sem, send_sem, chunk_send, chunk_recv, block_recv, ids_send, ids_recv, strip_send, ready_next, ready_strip, ready_wrap,
+    load_sem, id_sem, send_sem, chunk_send, chunk_recv, block_recv, ids_send, ids_recv, strip_send, ready_next, ready_strip, ready_wrap,
 ):
     g = lax.axis_index("group")
     k = lax.axis_index("blk")
@@ -60,12 +62,19 @@
     tell(partner)
 
     loads = []
+    id_loads = [
+        pltpu.make_async_copy(src, id_rows.at[a], id_sem.at[a])
+        for a, src in enumerate((text_ids, image_ids))
+    ]
     for c in range(N_CHUNK):
         for a, (src, dst) in enumerate(((texts, tx), (images, im))):
             rows = pl.ds(c * CHUNK, CHUNK)
             copy = pltpu.make_async_copy(src.at[rows], dst.at[rows], load_sem.at[a, c])
             copy.start()
             loads.append(copy)
+        if c == 0:
+            for copy in id_loads:
+                copy.start()
 
     @pl.when(jnp.logical_not(last))
     def _():
@@ -84,11 +93,6 @@
         for s in range(1, N_Z):
             tell(at(yhi, s, core))
 
-    ids[...] = jnp.concatenate(
-        [text_ids[...], image_ids[...], jnp.zeros((6, ROWS), jnp.int32)], axis=0
-    )
-    col_t[...] = jnp.broadcast_to(text_ids[...].astype(F32), (128, ROWS)).T
-    col_i[...] = jnp.broadcast_to(image_ids[...].astype(F32), (128, ROWS)).T
     scale = jnp.exp(jnp.full((1, 1), log_scale[0], F32))
     offset = bias[0]
 
@@ -117,16 +121,16 @@
                       send_sem.at[2 + part], block_recv.at[1], k_prev)
 
     def strip_text(s):
-        return remote(rows_of(th, s * STRIP, STRIP), relay_t, strip_send.at[s], block_recv.at[2], at(yhi, s, core))
+        return remote(rows_of(th, (s + 1) * STRIP, STRIP), relay_t, strip_send.at[s], block_recv.at[2], at(yhi, s, core))
 
     def strip_image(s):
         return remote(rows_of(ih, s * STRIP, STRIP), relay_i, strip_send.at[s], block_recv.at[3], at(yhi, s, core))
 
     mine = pl.multiple_of(z * STRIP, STRIP)
-    pass_text = remote(relay_t, rows_of(t2, mine, STRIP), send_sem.at[4], block_recv.at[0], wrap_next)
+    after = pl.multiple_of(lax.rem(z + 1, N_Z) * STRIP, STRIP)
+    pass_text = remote(relay_t, rows_of(t2, after, STRIP), send_sem.at[4], block_recv.at[0], wrap_next)
     pass_image = remote(relay_i, rows_of(i2, mine, STRIP), send_sem.at[5], block_recv.at[1], wrap_prev)
-    end = (N_Z - 1) * STRIP
-    own_text = remote(rows_of(th, end, STRIP), rows_of(t2, end, STRIP), send_sem.at[4], block_recv.at[0], wrap_next)
+    own_text = remote(rows_of(th, 0, STRIP), rows_of(t2, 0, STRIP), send_sem.at[4], block_recv.at[0], wrap_next)
     own_image = remote(rows_of(ih, 0, STRIP), rows_of(i2, 0, STRIP), send_sem.at[5], block_recv.at[1], wrap_prev)
 
     core_text = remote(th, t1, send_sem.at[6], block_recv.at[4], partner)
@@ -156,16 +160,17 @@
             pl.semaphore_wait(
                 barrier, 4 + 2 * (z > 0).astype(jnp.int32) + 15 * last.astype(jnp.int32)
             )
-        if c < 2:
-            group_text(c).start()
 
         @pl.when(last)
         def _():
-            for s in range(c * CHUNK // STRIP, (c + 1) * CHUNK // STRIP):
-                if s < N_Z - 1:
-                    strip_text(s).start()
-                else:
-                    own_text.start()
+            if c == 0:
+                own_text.start()
+            for r in range(c * CHUNK // STRIP, (c + 1) * CHUNK // STRIP):
+                if r > 0:
+                    strip_text(r - 1).start()
+
+        if c < N_FIRST_TEXT:
+            group_text(c).start()
 
         if c == 0:
             @pl.when(z > 0)
@@ -180,9 +185,16 @@
 
         loads[2 * c + 1].wait()
         normalize(c, im, ih, inv_i)
-        if c < 2:
+        if c < N_FIRST_IMAGE:
             group_image(c).start()
 
+    for copy in id_loads:
+        copy.wait()
+    ids[...] = jnp.concatenate(
+        [id_rows[0], id_rows[1], jnp.zeros((6, ROWS), jnp.int32)], axis=0
+    )
+    col_t[...] = jnp.broadcast_to(id_rows[0].astype(F32), (128, ROWS)).T
+    col_i[...] = jnp.broadcast_to(id_rows[1].astype(F32), (128, ROWS)).T
     for copy in ids_copies:
         copy.start()
 
@@ -231,13 +243,10 @@
             terms = jnp.broadcast_to(terms, (ROWS, 128))
             loss[...] = terms if fresh else loss[...] + terms
 
-        def add(t, carry):
-            cols = pl.ds(pl.multiple_of(t * TILE, 128), TILE)
+        for t in range(0, D, TILE):
+            cols = pl.ds(t, TILE)
             term = jnp.dot(coeff, other[pl.ds(start, count), cols], preferred_element_type=F32)
             acc[:, cols] = term if fresh else acc[:, cols] + term
-            return carry
-
-        lax.fori_loop(0, D // TILE, add, 0)
 
     def image_side(block, text_row, start=0, count=ROWS, fresh=False):
         side(ih, col_i, block, start, count, text_row, acc_i, loss_acc, fresh)
@@ -274,6 +283,14 @@
             pl.semaphore_wait(ready_strip.at[s], 1)
             strip_image(s).start()
 
+    @pl.when(jnp.logical_not(last))
+    def _():
+        strip_text(0).wait_recv()
+        pass_text.start()
+
+    for c in range(N_FIRST_TEXT, N_CHUNK):
+        group_text(c).start()
+
     @pl.when(z > 0)
     def _():
         strip_image(0).wait_recv()
@@ -291,72 +308,67 @@
         own_image.start()
         ids_prev.start()
 
-    for c in range(2, N_CHUNK):
+    for c in range(N_FIRST_IMAGE, N_CHUNK):
         group_image(c).start()
-
-    @pl.when(jnp.logical_not(last))
-    def _():
-        strip_text(0).wait_recv()
-        pass_text.start()
-
-    for c in range(2, N_CHUNK):
-        group_text(c).start()
 
     whole_text = remote(th, t2, send_sem.at[0], block_recv.at[0], k_next)
     whole_image = remote(ih, i2, send_sem.at[2], block_recv.at[1], k_prev)
-    ids_prev.wait_recv()
-    whole_image.wait_recv()
-
-    @pl.when(core == 0)
-    def _():
-        ids_on_image.start()
-        on_image.start()
-
-    text_side(i2, ids_in[3, 1:2, :])
-    ids_next.wait_recv()
-    whole_text.wait_recv()
-
-    @pl.when(core == 1)
-    def _():
-        ids_on_text.start()
-        on_text.start()
-
-    image_side(t2, ids_in[2, 0:1, :])
-    ids_on_text.wait_recv()
-
-    @pl.when(core == 0)
-    def _():
+
+    def meet_image():
+        ids_prev.wait_recv()
+        whole_image.wait_recv()
+
+        @pl.when(core == 0)
+        def _():
+            ids_on_image.start()
+            on_image.start()
+
+        text_side(i2, ids_in[3, 1:2, :])
+
+    def meet_text():
+        ids_next.wait_recv()
+        whole_text.wait_recv()
+
+        @pl.when(core == 1)
+        def _():
+            ids_on_text.start()
+            on_text.start()
+
+        image_side(t2, ids_in[2, 0:1, :])
+
+    def meet_passed_text():
+        ids_on_text.wait_recv()
         on_text.wait_recv()
         image_side(t1, ids_in[5, 0:1, :])
 
-    @pl.when(core == 1)
-    def _():
+    def meet_passed_image():
+        ids_on_image.wait_recv()
         on_image.wait_recv()
         text_side(i1, ids_in[5, 1:2, :])
 
+    pl.when(jnp.logical_not(last))(meet_image)
+    pl.when(jnp.logical_not(first))(meet_text)
+    pl.when(jnp.logical_not(last) & (core == 1))(meet_passed_image)
+    pl.when(jnp.logical_not(first) & (core == 0))(meet_passed_text)
+
     ids_copies[0].wait_recv()
     ids_copies[1].wait_recv()
-    for c in range(N_CHUNK):
-        here = c * CHUNK
-        group_text(c).wait_recv()
-        image_side(tg, ids_in[0, 0:1, here:here + CHUNK], here, CHUNK)
-        group_image(c).wait_recv()
-        text_side(ig, ids_in[1, 1:2, here:here + CHUNK], here, CHUNK)
-
-    def backward(raw, inv_ref, acc, out):
-        def step(r, carry):
-            rows = pl.ds(pl.multiple_of(r * 32, 32), 32)
-            inv = inv_ref[rows, 0:1]
-            unit = raw[rows, :] * inv
-            grad = acc[rows, :]
-            out[rows, :] = inv * (grad - unit * jnp.sum(unit * grad, axis=-1, keepdims=True))
-            return carry
-
-        lax.fori_loop(0, ROWS // 32, step, 0)
-
-    backward(im, inv_i, acc_i, image_out)
-    backward(tx, inv_t, acc_t, text_out)
-    loss_out[...] = loss_acc[...].T[0:1, :]
+
+    def meet_group(begin, stop):
+        here, count = begin * CHUNK, (stop - begin) * CHUNK
+        for c in range(begin, stop):
+            group_text(c).wait_recv()
+        image_side(tg, ids_in[0, 0:1, here:here + count], here, count)
+        for c in range(begin, stop):
+            group_image(c).wait_recv()
+        text_side(ig, ids_in[1, 1:2, here:here + count], here, count)
+
+    meet_group(0, N_CHUNK - 1)
+    pl.when(last)(meet_image)
+    pl.when(first)(meet_text)
+    pl.when(last & (core == 1))(meet_passed_image)
+    pl.when(first & (core == 0))(meet_passed_text)
+    meet_group(N_CHUNK - 1, N_CHUNK)
 
     for c in range(N_CHUNK):
         group_text(c).wait_send()
@@ -393,36 +405,65 @@
             strip_image(s).wait_send()
 
 
+def finish(im, tx, inv_i, inv_t, acc_i, acc_t, loss_acc, loss_out, image_out, text_out, row, image_buf, text_buf, sems):
+    row[...] = loss_acc[...].T[0:1, :]
+    loss_copy = pltpu.make_async_copy(row, loss_out, sems.at[2, 0])
+    loss_copy.start()
+    copies = [loss_copy]
+    for a, (raw, inv_ref, acc, buf, out) in enumerate(
+        ((im, inv_i, acc_i, image_buf, image_out), (tx, inv_t, acc_t, text_buf, text_out))
+    ):
+        for c in range(N_CHUNK):
+            rows = pl.ds(c * CHUNK, CHUNK)
+            inv = inv_ref[rows, 0:1]
+            unit = raw[rows, :] * inv
+            grad = acc[rows, :]
+            buf[rows, :] = inv * (grad - unit * jnp.sum(unit * grad, axis=-1, keepdims=True))
+            copy = pltpu.make_async_copy(buf.at[rows], out.at[rows], sems.at[a, c])
+            copy.start()
+            copies.append(copy)
+    for copy in copies:
+        copy.wait()
+
+
 def local(images, texts, image_ids, text_ids, log_scale, bias):
     block = pltpu.VMEM((ROWS, D), BF16)
     wide = pltpu.VMEM((ROWS, D), F32)
     lanes = pltpu.VMEM((ROWS, 128), F32)
+    wide_out = jax.ShapeDtypeStruct((ROWS, D), F32)
+    lanes_out = jax.ShapeDtypeStruct((ROWS, 128), F32)
     dma, plain = pltpu.SemaphoreType.DMA, pltpu.SemaphoreType.REGULAR
     vmem = pl.BlockSpec(memory_space=pltpu.VMEM)
     smem = pl.BlockSpec(memory_space=pltpu.SMEM)
-    hbm = pl.BlockSpec(memory_space=pl.ANY)
-    row_loss, image_grad, text_grad = pl.pallas_call(
+    hbm = pl.BlockSpec(memory_space=pltpu.HBM)
+    given = (images, texts, image_ids.reshape(1, ROWS), text_ids.reshape(1, ROWS))
+    in_hbm = [pltpu.with_memory_space_constraint(a, pltpu.HBM) for a in given]
+    parts = pl.pallas_call(
         kernel,
-        out_shape=(
-            jax.ShapeDtypeStruct((1, ROWS), F32),
-            jax.ShapeDtypeStruct((ROWS, D), F32),
-            jax.ShapeDtypeStruct((ROWS, D), F32),
-        ),
-        in_specs=[hbm, hbm, vmem, vmem, smem, smem],
-        out_specs=(vmem, vmem, vmem),
+        out_shape=(wide_out, wide_out, lanes_out, lanes_out, wide_out, wide_out, lanes_out),
+        in_specs=[hbm, hbm, hbm, hbm, smem, smem],
+        out_specs=(vmem,) * 7,
         scratch_shapes=[
-            wide, wide, block, block, lanes, lanes, wide, wide, lanes, lanes, lanes,
+            block, block, lanes, lanes, pltpu.VMEM((2, 1, ROWS), jnp.int32),
             pltpu.VMEM((8, ROWS), jnp.int32),
             block, block, block, block, block, block,
             pltpu.VMEM((STRIP, D), BF16), pltpu.VMEM((STRIP, D), BF16),
             pltpu.VMEM((6, 8, ROWS), jnp.int32),
-            dma((2, N_CHUNK)), dma((8,)), dma((2, N_CHUNK)), dma((2, N_CHUNK)), dma((6,)),
+            dma((2, N_CHUNK)), dma((2,)), dma((8,)), dma((2, N_CHUNK)), dma((2, N_CHUNK)), dma((6,)),
             dma((6,)), dma((6,)), dma((N_Z,)), plain, plain((N_Z,)), plain,
         ],
         compiler_params=pltpu.CompilerParams(
-            collective_id=0, has_side_effects=True, vmem_limit_bytes=48 * 1024 * 1024
+            collective_id=0, has_side_effects=True, vmem_limit_bytes=32 * 1024 * 1024
         ),
-    )(images, texts, image_ids.reshape(1, ROWS), text_ids.reshape(1, ROWS), log_scale, bias)
+    )(*in_hbm, log_scale, bias)
+    row_loss, image_grad, text_grad = pl.pallas_call(
+        finish,
+        out_shape=(jax.ShapeDtypeStruct((1, ROWS), F32), wide_out, wide_out),
+        in_specs=[vmem] * 7,
+        out_specs=(hbm,) * 3,
+        scratch_shapes=[pltpu.VMEM((1, ROWS), F32), wide, wide, dma((3, N_CHUNK))],
+        compiler_params=pltpu.CompilerParams(vmem_limit_bytes=16 * 1024 * 1024),
+    )(*parts)
     return row_loss.reshape(ROWS), image_grad, text_grad
 
 

time: 65.3 us -> 45 us (0.69)
  Pallas kernels: 56.6 us -> 42.7 us
  local copies, waits for them, and re-layouts: 6.48 us -> 0 us
    pallas_call x1 -> x2, Pallas kernels: 56.6 us -> 42.7 us  [the longest x1 40.4 us: local(): pl.pallas_call(kernel, out_shape=(wide_out, wide_out, lanes_out, lanes_ou...]
    unnamed x11 -> x0, local copies, waits for them, and re-layouts: 6.48 us -> none
where the time goes in v2:
time: 45 us; the launch traced here: 44.8 us
  Pallas kernels  42.7 us (95%)
  between operations  2.09 us (5%)
    pallas_call x1, Pallas kernels, local(): pl.pallas_call(kernel, out_shape=(wide_out, wide_out, lanes_out, lanes_ou...  40.4 us
    pallas_call x1, Pallas kernels, local(): pl.pallas_call(finish, out_shape=(jax.ShapeDtypeStruct((1, ROWS), F32), w...  2.33 us

profile of v2, /device:TPU:6, one launch (start us, length us, event | category | flops | bytes accessed | tf_op | source)
XLA Modules:
  0.0 44.8 jit_solution(14519120612310664630)
XLA Ops:
  1.9 40.4 %shard_map.85 = (f32[256,1152]{1,0:T(8,128)S(1)}, f32[256,1152]{1,0:T(8,128)S(1)}, f32[256,128]{1,0:T(8,128)S(1)}, f32[256,128]{1,0:T(8,128)S(1)}, f32[256,1152]...) custom-call(f32[256,1152]{1,0:T(8,128)} %images.1, f32[256,1152]{1,0:T(8,128)} %texts.1, ...), custom_call_target="tpu_custom_call" | custom-call | tf_op jit(solution)/shard_map/pallas_call | solution.py:441
  42.3 2.3 %shard_map.86 = (f32[1,256]{1,0:T(1,128)}, f32[256,1152]{1,0:T(8,128)}, f32[256,1152]{1,0:T(8,128)}) custom-call(f32[256,1152]{1,0:T(8,128)S(1)} %get-tuple-element.13.im, f32[256,1152]{1,0:T(8,128)S(1)} %get-tuple-element.14.tx, f32[256,128]{1,0:T(8,128)S(1)} %get-tuple-element.15.inv_i, f32[256,128]{1,0:T(8,128)S(1)} %get-tuple-element.16.inv_t, ...), custom_call_target="tpu_custom_call" | custom-call | tf_op jit(solution)/shard_map/pallas_call | solution.py:459

commit v3 on v2

v3 whole, which is shorter than its diff:
```python
import functools

import jax
import jax.numpy as jnp
from jax import lax
from jax.experimental import pallas as pl
from jax.experimental.pallas import tpu as pltpu
from jax.sharding import PartitionSpec as P

MESH = pl.DeviceIdType.MESH
ROWS = 256
D = 1152
N_Z = 8
N_YHI = 4
N_GROUP = 8
STRIP = ROWS // N_Z
CHUNK = 64
N_CHUNK = ROWS // CHUNK
N_EARLY = 3
TILE = 384
F32 = jnp.float32
BF16 = jnp.bfloat16


def rows_of(ref, start, count):
    return ref.at[pl.ds(start, count)]


def backward(raw, inv, grad):
    unit = raw * inv
    return inv * (grad - unit * jnp.sum(unit * grad, axis=-1, keepdims=True))


def kernel(
    images, texts, image_ids, text_ids, log_scale, bias,
    tx, inv_t, image_grad, acc_t, loss_acc,
    im, inv_i, acc_i, ih, th, col_i, col_t, id_rows, ids,
    t1, t2, tg, i1, i2, ig, relay_t, relay_i, ids_in,
    load_sem, id_sem, send_sem, chunk_send, chunk_recv, block_recv, two_recv, pass_send, pass_recv, next_send, prev_send, ids_send, ids_recv, strip_send, ready_next, ready_strip, ready_wrap,
):
    g = lax.axis_index("group")
    k = lax.axis_index("blk")
    core = lax.rem(k, 2)
    z = lax.rem(k // 2, N_Z)
    yhi = k // (2 * N_Z)
    first, last = z == 0, z == N_Z - 1

    even = 2 * (1 - lax.rem(g, 2))
    relay_g = lax.rem(g + N_GROUP - even, N_GROUP)
    from_g = lax.rem(g + even, N_GROUP)

    def at(yh, zz, cc, gg=g):
        return (gg, (lax.rem(yh + N_YHI, N_YHI) * N_Z + zz) * 2 + cc)

    g_next = (lax.rem(g + 1, N_GROUP), k)
    g_prev = (lax.rem(g + N_GROUP - 1, N_GROUP), k)
    partner = (g, k + 1 - 2 * core)
    wrap_next = at(yhi + 1, 0, core)
    wrap_prev = at(yhi - 1, N_Z - 1, core)
    k_next = (g, lax.rem(k + 2, 2 * N_Z * N_YHI))
    k_prev = (g, lax.rem(k + 2 * N_Z * N_YHI - 2, 2 * N_Z * N_YHI))

    barrier = pltpu.get_barrier_semaphore()

    def tell(device):
        pl.semaphore_signal(barrier, inc=1, device_id=device, device_id_type=MESH)

    tell(g_next)
    tell(g_prev)
    tell(partner)

    loads = []
    id_loads = [
        pltpu.make_async_copy(src, id_rows.at[a], id_sem.at[a])
        for a, src in enumerate((text_ids, image_ids))
    ]
    for a, (src, dst) in enumerate(((texts, tx), (images, im))):
        for c in range(N_CHUNK):
            rows = pl.ds(c * CHUNK, CHUNK)
            copy = pltpu.make_async_copy(src.at[rows], dst.at[rows], load_sem.at[a, c])
            loads.append(copy)
    for copy in loads[:N_CHUNK] + id_loads:
        copy.start()

    @pl.when(jnp.logical_not(last))
    def _():
        tell(k_next)
        tell(at(yhi, N_Z - 1, core, from_g))
        tell(wrap_prev)

    @pl.when(last)
    def _():
        tell(at(yhi + 1, N_Z - 1, core))

    @pl.when(first)
    def _():
        tell(wrap_prev)
        for s in range(N_Z - 1):
            tell(at(yhi - 1, s, core, relay_g))
        for s in range(1, N_Z):
            tell(at(yhi, s, core))

    scale = jnp.exp(jnp.full((1, 1), log_scale[0], F32))
    offset = bias[0]

    def remote(src, dst, send, recv, device):
        return pltpu.make_async_remote_copy(
            src_ref=src, dst_ref=dst, send_sem=send, recv_sem=recv,
            device_id=device, device_id_type=MESH,
        )

    def group_text(c):
        return remote(rows_of(th, c * CHUNK, CHUNK), rows_of(tg, c * CHUNK, CHUNK),
                      chunk_send.at[0, c], chunk_recv.at[0, c], g_next)

    def group_image(c):
        return remote(rows_of(ih, c * CHUNK, CHUNK), rows_of(ig, c * CHUNK, CHUNK),
                      chunk_send.at[1, c], chunk_recv.at[1, c], g_prev)

    def next_text(part):
        return remote(rows_of(th, part * CHUNK, CHUNK), rows_of(t2, part * CHUNK, CHUNK),
                      next_send.at[part], two_recv.at[0, part], k_next)

    def prev_image(part):
        return remote(rows_of(ih, part * CHUNK, CHUNK), rows_of(i2, part * CHUNK, CHUNK),
                      prev_send.at[part], two_recv.at[1, part], k_prev)

    def strip_text(s):
        return remote(rows_of(th, (s + 1) * STRIP, STRIP), relay_t, strip_send.at[s], block_recv.at[2], at(yhi, s, core, relay_g))

    def strip_image(s):
        return remote(rows_of(ih, s * STRIP, STRIP), relay_i, strip_send.at[s], block_recv.at[3], at(yhi, s, core))

    mine = pl.multiple_of(z * STRIP, STRIP)
    after = pl.multiple_of(lax.rem(z + 1, N_Z) * STRIP, STRIP)
    pass_text = remote(relay_t, rows_of(t2, after, STRIP), send_sem.at[4], two_recv.at[0, after // CHUNK], at(yhi + 1, 0, core, from_g))
    pass_image = remote(relay_i, rows_of(i2, mine, STRIP), send_sem.at[5], two_recv.at[1, mine // CHUNK], wrap_prev)
    own_text = remote(rows_of(th, 0, STRIP), rows_of(t2, 0, STRIP), send_sem.at[4], two_recv.at[0, 0], wrap_next)
    own_image = remote(rows_of(ih, 0, STRIP), rows_of(i2, 0, STRIP), send_sem.at[5], two_recv.at[1, 0], wrap_prev)

    core_text = remote(th, t1, send_sem.at[6], block_recv.at[4], partner)
    core_image = remote(ih, i1, send_sem.at[6], block_recv.at[5], partner)

    def on_text(part):
        return remote(rows_of(t2, part * CHUNK, CHUNK), rows_of(t1, part * CHUNK, CHUNK),
                      pass_send.at[part], pass_recv.at[part], partner)

    def on_image(part):
        return remote(rows_of(i2, part * CHUNK, CHUNK), rows_of(i1, part * CHUNK, CHUNK),
                      pass_send.at[part], pass_recv.at[part], partner)

    def send_ids(slot, device, src=ids):
        return remote(src, ids_in.at[slot], ids_send.at[slot], ids_recv.at[slot], device)

    ids_next, ids_prev = send_ids(2, k_next), send_ids(3, k_prev)
    ids_copies = [send_ids(0, g_next), send_ids(1, g_prev), send_ids(4, partner)]
    ids_on_text = send_ids(5, partner, ids_in.at[2])
    ids_on_image = send_ids(5, partner, ids_in.at[3])

    def normalize(c, raw, half_ref, inv_ref):
        rows = pl.ds(c * CHUNK, CHUNK)
        values = raw[rows, :]
        inv = lax.rsqrt(jnp.sum(values * values, axis=-1, keepdims=True) + 1e-06)
        half_ref[rows, :] = (values * inv).astype(BF16)
        inv_ref[rows, :] = jnp.broadcast_to(inv, (CHUNK, 128))

    for c in range(N_CHUNK):
        loads[c].wait()
        if c == 0:
            for copy in loads[N_CHUNK:]:
                copy.start()
        normalize(c, tx, th, inv_t)
        if c == 0:
            pl.semaphore_wait(
                barrier, 4 + 2 * (z > 0).astype(jnp.int32) + 15 * last.astype(jnp.int32)
            )

        @pl.when(last)
        def _():
            if c == 0:
                own_text.start()
            for r in range(c * CHUNK // STRIP, (c + 1) * CHUNK // STRIP):
                if r > 0:
                    strip_text(r - 1).start()

        group_text(c).start()
        if c == 0:
            @pl.when(z > 0)
            def _():
                pl.semaphore_signal(ready_next, inc=1, device_id=k_prev, device_id_type=MESH)
                pl.semaphore_signal(ready_strip.at[z], inc=1, device_id=at(yhi, 0, core), device_id_type=MESH)

            @pl.when(last)
            def _():
                for s in range(N_Z - 1):
                    pl.semaphore_signal(ready_wrap, inc=1, device_id=at(yhi + 1, s, core), device_id_type=MESH)

    @pl.when(core == 0)
    def _():
        core_text.start()

    @pl.when(jnp.logical_not(last))
    def _():
        pl.semaphore_wait(ready_next, 1)
        next_text(0).start()
        next_text(1).start()

    @pl.when(jnp.logical_not(last) & (z > 0))
    def _():
        next_text(2).start()
        next_text(3).start()

    for c in range(N_CHUNK):
        loads[N_CHUNK + c].wait()
        normalize(c, im, ih, inv_i)
        pl.when(z > 0)(prev_image(c).start)

    @pl.when(core == 1)
    def _():
        core_image.start()

    for copy in id_loads:
        copy.wait()
    ids[...] = jnp.concatenate(
        [id_rows[0], id_rows[1], jnp.zeros((6, ROWS), jnp.int32)], axis=0
    )
    col_t[...] = jnp.broadcast_to(id_rows[0].astype(F32), (128, ROWS)).T
    col_i[...] = jnp.broadcast_to(id_rows[1].astype(F32), (128, ROWS)).T
    for copy in ids_copies:
        copy.start()

    ids_next.start()
    pl.when(z > 0)(ids_prev.start)

    def side(own_half, own_col, other, start, count, other_ids, acc, loss, fresh=False):
        block = other[pl.ds(start, count), :]
        dots = lax.dot_general(
            own_half[...], block, (((1,), (1,)), ((), ())), preferred_element_type=F32
        )
        logit = scale * dots + offset
        same = own_col[:, 0:1] == other_ids.astype(F32)
        u = jnp.where(same, -logit, logit)
        e = jnp.exp(-jnp.abs(u))
        coeff = jnp.where(same, -scale, scale) * (jnp.where(u >= 0, 1.0, e) / (1.0 + e))
        coeff = coeff.astype(BF16)
        if loss is not None:
            terms = jnp.maximum(u, 0.0) + jnp.log1p(e)
            terms = jnp.sum(terms, axis=1, keepdims=True)
            terms = jnp.broadcast_to(terms, (ROWS, 128))
            loss[...] = terms if fresh else loss[...] + terms

        for t in range(0, D, TILE):
            cols = pl.ds(t, TILE)
            term = jnp.dot(coeff, other[pl.ds(start, count), cols], preferred_element_type=F32)
            acc[:, cols] = term if fresh else acc[:, cols] + term

    def image_side(block, text_row, start=0, count=ROWS, fresh=False):
        side(ih, col_i, block, start, count, text_row, acc_i, loss_acc, fresh)

    def text_side(block, image_row, start=0, count=ROWS, fresh=False):
        side(th, col_t, block, start, count, image_row, acc_t, None, fresh)

    image_side(th, ids[0:1, :], fresh=True)

    @pl.when(first)
    def _():
        for s in range(1, 5):
            pl.semaphore_wait(ready_strip.at[s], 1)
            strip_image(s).start()
        next_text(2).start()
        next_text(3).start()

    text_side(ih, ids[1:2, :], fresh=True)

    send_ids(4, partner).wait_recv()

    @pl.when(core == 0)
    def _():
        core_image.wait_recv()
        text_side(i1, ids_in[4, 1:2, :])

    @pl.when(core == 1)
    def _():
        core_text.wait_recv()
        image_side(t1, ids_in[4, 0:1, :])

    @pl.when(first)
    def _():
        for s in range(5, N_Z):
            pl.semaphore_wait(ready_strip.at[s], 1)
            strip_image(s).start()

    @pl.when((z >= N_EARLY) & jnp.logical_not(last))
    def _():
        strip_text(0).wait_recv()
        pass_text.start()

    for c in range(N_CHUNK - 1):
        group_text(c).wait_send()
    group_image(0).start()

    @pl.when(z < N_EARLY)
    def _():
        strip_text(0).wait_recv()
        pass_text.start()

    group_image(1).start()

    def relay_image():
        @pl.when(z > 0)
        def _():
            strip_image(0).wait_recv()

        @pl.when(jnp.logical_not(last))
        def _():
            pl.semaphore_wait(ready_wrap, 1)

        pl.when(z > 0)(pass_image.start)

        @pl.when(first)
        def _():
            own_image.start()
            ids_prev.start()

        for c in range(2, N_CHUNK):
            group_image(c).start()

    def meet_image():
        ids_prev.wait_recv()
        pl.when(core == 0)(ids_on_image.start)
        for part in range(N_CHUNK):
            prev_image(part).wait_recv()
            pl.when(core == 0)(on_image(part).start)
        text_side(i2, ids_in[3, 1:2, :])

    def meet_text():
        ids_next.wait_recv()
        pl.when(core == 1)(ids_on_text.start)
        for part in range(N_CHUNK):
            next_text(part).wait_recv()
            pl.when(core == 1)(on_text(part).start)
        image_side(t2, ids_in[2, 0:1, :])

    def meet_passed_text():
        ids_on_text.wait_recv()
        for part in range(N_CHUNK):
            on_text(part).wait_recv()
        image_side(t1, ids_in[5, 0:1, :])

    def meet_passed_image():
        ids_on_image.wait_recv()
        for part in range(N_CHUNK):
            on_image(part).wait_recv()
        text_side(i1, ids_in[5, 1:2, :])

    pl.when((z < 2) | (z >= 6))(relay_image)
    pl.when(jnp.logical_not(first))(meet_text)
    pl.when((z >= 2) & (z < 6))(relay_image)
    pl.when(jnp.logical_not(last))(meet_image)
    pl.when(jnp.logical_not(last) & (core == 1))(meet_passed_image)
    pl.when(jnp.logical_not(first) & (core == 0))(meet_passed_text)

    ids_copies[0].wait_recv()
    ids_copies[1].wait_recv()
    for c in range(N_CHUNK):
        group_text(c).wait_recv()
    image_side(tg, ids_in[0, 0:1, :])

    def meet_group_image(begin, stop):
        here, count = begin * CHUNK, (stop - begin) * CHUNK
        for c in range(begin, stop):
            group_image(c).wait_recv()
        text_side(ig, ids_in[1, 1:2, here:here + count], here, count)

    def image_backward():
        for c in range(N_CHUNK):
            rows = pl.ds(c * CHUNK, CHUNK)
            image_grad[rows, :] = backward(im[rows, :], inv_i[rows, 0:1], acc_i[rows, :])

    pl.when(jnp.logical_not(first))(image_backward)
    pl.when(last & (core == 0))(meet_image)
    meet_group_image(0, N_CHUNK - 1)
    pl.when(first & (core == 1))(meet_text)
    pl.when(first & (core == 0))(meet_passed_text)
    pl.when(last & (core == 1))(meet_image)
    pl.when(last & (core == 1))(meet_passed_image)
    meet_group_image(N_CHUNK - 1, N_CHUNK)
    pl.when(first & (core == 0))(meet_text)
    pl.when(first)(image_backward)

    group_text(N_CHUNK - 1).wait_send()
    for c in range(N_CHUNK):
        group_image(c).wait_send()
    for copy in ids_copies:
        copy.wait_send()
    ids_next.wait_send()
    ids_prev.wait_send()
    ids_on_text.wait_send()
    core_text.wait_send()
    for part in range(N_CHUNK):
        on_text(part).wait_send()

    @pl.when(z > 0)
    def _():
        for part in range(N_CHUNK):
            prev_image(part).wait_send()

    @pl.when(jnp.logical_not(last))
    def _():
        for part in range(N_CHUNK):
            next_text(part).wait_send()

    pass_text.wait_send()
    pass_image.wait_send()

    @pl.when(last)
    def _():
        for s in range(N_Z - 1):
            strip_text(s).wait_send()

    @pl.when(first)
    def _():
        for s in range(1, N_Z):
            strip_image(s).wait_send()


def finish(tx, inv_t, image_grad, acc_t, loss_acc, loss_out, image_out, text_out, row, buf, sems):
    image_copy = pltpu.make_async_copy(image_grad, image_out, sems.at[N_CHUNK])
    image_copy.start()
    copies = [image_copy]
    for c in range(N_CHUNK):
        rows = pl.ds(c * CHUNK, CHUNK)
        buf[rows, :] = backward(tx[rows, :], inv_t[rows, 0:1], acc_t[rows, :])
        copy = pltpu.make_async_copy(buf.at[rows], text_out.at[rows], sems.at[c])
        copy.start()
        copies.append(copy)
    row[...] = loss_acc[...].T[0:1, :]
    loss_copy = pltpu.make_async_copy(row, loss_out, sems.at[N_CHUNK + 1])
    loss_copy.start()
    for copy in copies + [loss_copy]:
        copy.wait()


def local(images, texts, image_ids, text_ids, log_scale, bias):
    block = pltpu.VMEM((ROWS, D), BF16)
    wide = pltpu.VMEM((ROWS, D), F32)
    lanes = pltpu.VMEM((ROWS, 128), F32)
    wide_out = jax.ShapeDtypeStruct((ROWS, D), F32)
    lanes_out = jax.ShapeDtypeStruct((ROWS, 128), F32)
    dma, plain = pltpu.SemaphoreType.DMA, pltpu.SemaphoreType.REGULAR
    vmem = pl.BlockSpec(memory_space=pltpu.VMEM)
    smem = pl.BlockSpec(memory_space=pltpu.SMEM)
    hbm = pl.BlockSpec(memory_space=pltpu.HBM)
    given = (images, texts, image_ids.reshape(1, ROWS), text_ids.reshape(1, ROWS))
    in_hbm = [pltpu.with_memory_space_constraint(a, pltpu.HBM) for a in given]
    parts = pl.pallas_call(
        kernel,
        out_shape=(wide_out, lanes_out, wide_out, wide_out, lanes_out),
        in_specs=[hbm, hbm, hbm, hbm, smem, smem],
        out_specs=(vmem,) * 5,
        scratch_shapes=[
            wide, lanes, wide, block, block, lanes, lanes, pltpu.VMEM((2, 1, ROWS), jnp.int32),
            pltpu.VMEM((8, ROWS), jnp.int32),
            block, block, block, block, block, block,
            pltpu.VMEM((STRIP, D), BF16), pltpu.VMEM((STRIP, D), BF16),
            pltpu.VMEM((6, 8, ROWS), jnp.int32),
            dma((2, N_CHUNK)), dma((2,)), dma((8,)), dma((2, N_CHUNK)), dma((2, N_CHUNK)), dma((6,)),
            dma((2, N_CHUNK)), dma((N_CHUNK,)), dma((N_CHUNK,)), dma((N_CHUNK,)), dma((N_CHUNK,)), dma((6,)), dma((6,)), dma((N_Z,)), plain, plain((N_Z,)), plain,
        ],
        compiler_params=pltpu.CompilerParams(
            collective_id=0, has_side_effects=True, vmem_limit_bytes=32 * 1024 * 1024
        ),
    )(*in_hbm, log_scale, bias)
    row_loss, image_grad, text_grad = pl.pallas_call(
        finish,
        out_shape=(jax.ShapeDtypeStruct((1, ROWS), F32), wide_out, wide_out),
        in_specs=[vmem] * 5,
        out_specs=(hbm,) * 3,
        scratch_shapes=[pltpu.VMEM((1, ROWS), F32), wide, dma((N_CHUNK + 2,))],
        compiler_params=pltpu.CompilerParams(vmem_limit_bytes=16 * 1024 * 1024),
    )(*parts)
    return row_loss.reshape(ROWS), image_grad, text_grad


def solution(mesh):
    rows, wide = P(("group", "blk")), P(("group", "blk"), None)
    return jax.shard_map(
        local,
        mesh=mesh,
        in_specs=(wide, wide, rows, rows, P(), P()),
        out_specs=(rows, wide, wide),
        check_vma=False,
    )
```

time: 45 us -> 44.2 us (0.982)
  the two profiles are of different devices: /device:TPU:6 before, /device:TPU:14 now
where the time goes in v3:
time: 44.2 us; the launch traced here: 44 us
  Pallas kernels  41.9 us (95%)
  between operations  2.09 us (5%)
    pallas_call x1, Pallas kernels, local(): pl.pallas_call(kernel, out_shape=(wide_out, lanes_out, wide_out, wide_out...  40.5 us
    pallas_call x1, Pallas kernels, local(): pl.pallas_call(finish, out_shape=(jax.ShapeDtypeStruct((1, ROWS), F32), w...  1.45 us

profile of v3, /device:TPU:14, one launch (start us, length us, event | category | flops | bytes accessed | tf_op | source)
XLA Modules:
  0.0 44.0 jit_solution(6185303773354237428)
XLA Ops:
  1.9 40.5 %shard_map.85 = (f32[256,1152]{1,0:T(8,128)S(1)}, f32[256,128]{1,0:T(8,128)S(1)}, f32[256,1152]{1,0:T(8,128)S(1)}, f32[256,1152]{1,0:T(8,128)S(1)}, f32[256,128]{1,0:T(8,128)S(1)}) custom-call(f32[256,1152]{1,0:T(8,128)} %images.1, f32[256,1152]{1,0:T(8,128)} %texts.1, s32[1,256]{1,0:T(1,128)} %bitcast.3, s32[1,256]{1,0:T(1,128)} %bitcast.4, ...), custom_call_target="tpu_custom_call" | custom-call | tf_op jit(solution)/shard_map/pallas_call | solution.py:456
  42.4 1.5 %shard_map.86 = (f32[1,256]{1,0:T(1,128)}, f32[256,1152]{1,0:T(8,128)}, f32[256,1152]{1,0:T(8,128)}) custom-call(f32[256,1152]{1,0:T(8,128)S(1)} %get-tuple-element.11.tx, f32[256,128]{1,0:T(8,128)S(1)} %get-tuple-element.12.inv_t, f32[256,1152]{1,0:T(8,128)S(1)} %get-tuple-element.13.image_grad, f32[256,1152]{1,0:T(8,128)S(1)} %get-tuple-element.14.acc_t, ...), custom_call_target="tpu_custom_call" | custom-call | tf_op jit(solution)/shard_map/pallas_call | solution.py:474

commit v4 on v3

--- a/solution.py
+++ b/solution.py
@@ -45,12 +45,8 @@
     yhi = k // (2 * N_Z)
     first, last = z == 0, z == N_Z - 1
 
-    even = 2 * (1 - lax.rem(g, 2))
-    relay_g = lax.rem(g + N_GROUP - even, N_GROUP)
-    from_g = lax.rem(g + even, N_GROUP)
-
-    def at(yh, zz, cc, gg=g):
-        return (gg, (lax.rem(yh + N_YHI, N_YHI) * N_Z + zz) * 2 + cc)
+    def at(yh, zz, cc):
+        return (g, (lax.rem(yh + N_YHI, N_YHI) * N_Z + zz) * 2 + cc)
 
     g_next = (lax.rem(g + 1, N_GROUP), k)
     g_prev = (lax.rem(g + N_GROUP - 1, N_GROUP), k)
@@ -59,6 +55,8 @@
     wrap_prev = at(yhi - 1, N_Z - 1, core)
     k_next = (g, lax.rem(k + 2, 2 * N_Z * N_YHI))
     k_prev = (g, lax.rem(k + 2 * N_Z * N_YHI - 2, 2 * N_Z * N_YHI))
+
+    slow = (k == 0) & ((g == 0) | (g == N_GROUP - 1))
 
     barrier = pltpu.get_barrier_semaphore()
 
@@ -85,7 +83,7 @@
     @pl.when(jnp.logical_not(last))
     def _():
         tell(k_next)
-        tell(at(yhi, N_Z - 1, core, from_g))
+        tell(at(yhi, N_Z - 1, core))
         tell(wrap_prev)
 
     @pl.when(last)
@@ -96,7 +94,7 @@
     def _():
         tell(wrap_prev)
         for s in range(N_Z - 1):
-            tell(at(yhi - 1, s, core, relay_g))
+            tell(at(yhi - 1, s, core))
         for s in range(1, N_Z):
             tell(at(yhi, s, core))
 
@@ -126,14 +124,14 @@
                       prev_send.at[part], two_recv.at[1, part], k_prev)
 
     def strip_text(s):
-        return remote(rows_of(th, (s + 1) * STRIP, STRIP), relay_t, strip_send.at[s], block_recv.at[2], at(yhi, s, core, relay_g))
+        return remote(rows_of(th, (s + 1) * STRIP, STRIP), relay_t, strip_send.at[s], block_recv.at[2], at(yhi, s, core))
 
     def strip_image(s):
         return remote(rows_of(ih, s * STRIP, STRIP), relay_i, strip_send.at[s], block_recv.at[3], at(yhi, s, core))
 
     mine = pl.multiple_of(z * STRIP, STRIP)
     after = pl.multiple_of(lax.rem(z + 1, N_Z) * STRIP, STRIP)
-    pass_text = remote(relay_t, rows_of(t2, after, STRIP), send_sem.at[4], two_recv.at[0, after // CHUNK], at(yhi + 1, 0, core, from_g))
+    pass_text = remote(relay_t, rows_of(t2, after, STRIP), send_sem.at[4], two_recv.at[0, after // CHUNK], at(yhi + 1, 0, core))
     pass_image = remote(relay_i, rows_of(i2, mine, STRIP), send_sem.at[5], two_recv.at[1, mine // CHUNK], wrap_prev)
     own_text = remote(rows_of(th, 0, STRIP), rows_of(t2, 0, STRIP), send_sem.at[4], two_recv.at[0, 0], wrap_next)
     own_image = remote(rows_of(ih, 0, STRIP), rows_of(i2, 0, STRIP), send_sem.at[5], two_recv.at[1, 0], wrap_prev)
@@ -295,8 +293,11 @@
         strip_text(0).wait_recv()
         pass_text.start()
 
-    for c in range(N_CHUNK - 1):
-        group_text(c).wait_send()
+    @pl.when(jnp.logical_not(slow))
+    def _():
+        for c in range(N_CHUNK - 1):
+            group_text(c).wait_send()
+
     group_image(0).start()
 
     @pl.when(z < N_EARLY)
@@ -387,6 +388,11 @@
     meet_group_image(N_CHUNK - 1, N_CHUNK)
     pl.when(first & (core == 0))(meet_text)
     pl.when(first)(image_backward)
+
+    @pl.when(slow)
+    def _():
+        for c in range(N_CHUNK - 1):
+            group_text(c).wait_send()
 
     group_text(N_CHUNK - 1).wait_send()
     for c in range(N_CHUNK):

time: 44.2 us -> 44.2 us (level)
  no operation moved by 1% of the time
where the time goes in v4:
time: 44.2 us; the launch traced here: 44 us
  Pallas kernels  41.9 us (95%)
  between operations  2.09 us (5%)
    pallas_call x1, Pallas kernels, local(): pl.pallas_call(kernel, out_shape=(wide_out, lanes_out, wide_out, wide_out...  40.5 us
    pallas_call x1, Pallas kernels, local(): pl.pallas_call(finish, out_shape=(jax.ShapeDtypeStruct((1, ROWS), F32), w...  1.45 us

profile of v4, /device:TPU:14, one launch (start us, length us, event | category | flops | bytes accessed | tf_op | source)
XLA Modules:
  0.0 44.0 jit_solution(3116762748525966536)
XLA Ops:
  1.9 40.5 %shard_map.85 = (f32[256,1152]{1,0:T(8,128)S(1)}, f32[256,128]{1,0:T(8,128)S(1)}, f32[256,1152]{1,0:T(8,128)S(1)}, f32[256,1152]{1,0:T(8,128)S(1)}, f32[256,128]{1,0:T(8,128)S(1)}) custom-call(f32[256,1152]{1,0:T(8,128)} %images.1, f32[256,1152]{1,0:T(8,128)} %texts.1, s32[1,256]{1,0:T(1,128)} %bitcast.3, s32[1,256]{1,0:T(1,128)} %bitcast.4, ...), custom_call_target="tpu_custom_call" | custom-call | tf_op jit(solution)/shard_map/pallas_call | solution.py:462
  42.4 1.5 %shard_map.86 = (f32[1,256]{1,0:T(1,128)}, f32[256,1152]{1,0:T(8,128)}, f32[256,1152]{1,0:T(8,128)}) custom-call(f32[256,1152]{1,0:T(8,128)S(1)} %get-tuple-element.11.tx, f32[256,128]{1,0:T(8,128)S(1)} %get-tuple-element.12.inv_t, f32[256,1152]{1,0:T(8,128)S(1)} %get-tuple-element.13.image_grad, f32[256,1152]{1,0:T(8,128)S(1)} %get-tuple-element.14.acc_t, ...), custom_call_target="tpu_custom_call" | custom-call | tf_op jit(solution)/shard_map/pallas_call | solution.py:480
